TPU v7x, 512 devices: a whole 4x8x8 slice. The times are simulated.
512 devices in a mesh: ctx: 8 (over y), zero: 64 (over x, z, core).
Axes of the slice: x: 4, y: 8, z: 8, core: 2. Of those that a mesh axis runs over, the one named last changes fastest.
Arguments:
- logit_partial: float32 [8, 8, 64], P('ctx'), may hold values from 10 to 400
- head_order: int32 [8, 64], replicated, may hold values from 0 to 63, each once within a row
- query_weight: float32 [8, 1536, 12288], P('ctx', 'zero'), may hold values from -0.15625 to 0.15625
- query_moment: bfloat16 [8, 1536, 12288], P('ctx', 'zero'), may hold values from -6 to 6
- query_grad: bfloat16 [8, 1536, 12288], P('ctx', 'zero'), may hold values from -6 to 6
- key_weight: float32 [8, 512, 8192], P('ctx', 'zero'), may hold values from -0.25 to 0.25
- key_moment: bfloat16 [8, 512, 8192], P('ctx', 'zero'), may hold values from -6 to 6
- key_grad: bfloat16 [8, 512, 8192], P('ctx', 'zero'), may hold values from -6 to 6
Outputs:
- query_final: float32 [8, 1536, 12288], P('ctx', 'zero')
- query_velocity: bfloat16 [8, 1536, 12288], P('ctx', 'zero')
- key_final: float32 [8, 512, 8192], P('ctx', 'zero')
- key_velocity: bfloat16 [8, 512, 8192], P('ctx', 'zero')
Inputs may be any that keep to these rules, and one draw needn't show every extreme that they name: `head_order`: each layer's row is a permutation of the 64 head numbers.
All inputs are finite; a program needn't handle non-finite values.
Results may differ from a plain program's by a relative error of at most 0.001.
Values may be sent and summed in bfloat16 or wider, within the bound.
A program may use at most 64 MiB of HBM per device.

v0:
```python
import functools
import math

import jax
import jax.numpy as jnp
from jax import lax
from jax.experimental import pallas as pl
from jax.experimental.pallas import tpu as pltpu
from jax.sharding import PartitionSpec as P

QR = 1536
KR = 512
NOPE = 128
ROPE = 64
WIDTH = NOPE + ROPE
ITERS = 5
LANES = 128
ROWS = 48


MOMENTUM_DECAY = 0.95
LEARN_RATE = 0.02
WEIGHT_DECAY = 0.1
CLIP_LIMIT = 100.0
NEWTON_FIRST = 3.4445
NEWTON_SECOND = -4.775
NEWTON_THIRD = 2.0315
NORM_EPSILON = 1e-07
HIGHEST = lax.Precision.HIGHEST
MESH = pl.DeviceIdType.MESH


def gram_of(x):
    return lax.dot_general(x, x, (((0,), (0,)), ((), ())), preferred_element_type=jnp.float32)


def mul(a, b):
    return lax.dot_general(
        a, b, (((1,), (0,)), ((), ())), precision=HIGHEST, preferred_element_type=jnp.float32
    )


def low_dot(x, high, low):
    return jnp.dot(x, high, preferred_element_type=jnp.float32) + jnp.dot(
        x, low, preferred_element_type=jnp.float32
    )


def begin(gram):
    size = gram.shape[0]
    eye = lax.broadcasted_iota(jnp.int32, (size, size), 0) == lax.broadcasted_iota(
        jnp.int32, (size, size), 1
    )
    total = jnp.sum(jnp.where(eye, gram, 0.0))
    inverse = 1.0 / (jnp.sqrt(jnp.full((1, 1), total)) + NORM_EPSILON)
    return gram * inverse * inverse, inverse, jnp.where(eye, 1.0, 0.0)


def newton(gram_q, gram_k):
    aq, iq, eq = begin(gram_q)
    ak, ik, ek = begin(gram_k)
    mq = mk = None
    for sweep in range(ITERS):
        sq, sk = mul(aq, aq), mul(ak, ak)
        pq = NEWTON_FIRST * eq + NEWTON_SECOND * aq + NEWTON_THIRD * sq
        pk = NEWTON_FIRST * ek + NEWTON_SECOND * ak + NEWTON_THIRD * sk
        if sweep == 0:
            mq, mk = pq, pk
        else:
            mq, mk = mul(mq, pq), mul(mk, pk)
        if sweep < ITERS - 1:
            yq, yk = mul(aq, pq), mul(ak, pk)
            aq, ak = mul(yq, pq), mul(yk, pk)
    return mq * iq, mk * ik


def split(m):
    high = m.astype(jnp.bfloat16)
    return high, (m - high.astype(jnp.float32)).astype(jnp.bfloat16)


def half_roll(x):
    return pltpu.roll(x, ROPE, 1)


def body(
    owners,
    n_ctx,
    lp_ref,
    order_ref,
    qw_hbm,
    qm_ref,
    qg_ref,
    kw_hbm,
    km_ref,
    kg_ref,
    qf_ref,
    qv_ref,
    kf_ref,
    kv_ref,
    send,
    recv,
    back,
    home,
    wide,
    gram_q,
    gram_k,
    lsend,
    lrecv,
    gamma,
    root,
    qw_ref,
    kw_ref,
    send_sem,
    recv_sem,
    back_sem,
    home_sem,
    lsend_sem,
    lrecv_sem,
    load_sem,
):
    nx = 4 if owners == 64 else 1
    chips = owners // 2
    nz = chips // nx
    group = 8 if owners == 64 else 4
    groups = owners // group
    pairs = group // 2
    me_c = lax.axis_index("ctx")
    me = lax.axis_index("zero")
    core = lax.rem(me, 2)
    chip = lax.div(me, 2)
    x0, z0 = lax.div(chip, nz), lax.rem(chip, nz)

    def offset(t):
        i = lax.rem(t, nz)
        dz = lax.div(i + 1, 2) * (1 - 2 * lax.rem(i + 1, 2))
        dx = lax.rem(t + lax.div(t, nz), nx)
        return dx, dz

    def chip_to(t):
        dx, dz = offset(t)
        return lax.rem(x0 + dx, nx) * nz + lax.rem(z0 + dz + nz, nz)

    def chip_from(t):
        dx, dz = offset(t)
        return lax.rem(x0 - dx + nx, nx) * nz + lax.rem(z0 - dz + nz, nz)

    def core_at(dc):
        return lax.rem(core + dc, 2)

    load_q = pltpu.make_async_copy(qw_hbm, qw_ref, load_sem.at[0])
    load_k = pltpu.make_async_copy(kw_hbm, kw_ref, load_sem.at[1])
    load_q.start()
    load_k.start()

    barrier = pltpu.get_barrier_semaphore()

    @pl.loop(1, owners)
    def _(i):
        pl.semaphore_signal(
            barrier, inc=1, device_id=(me_c, lax.rem(me + i, owners)), device_id_type=MESH
        )

    @pl.loop(1, n_ctx)
    def _(i):
        pl.semaphore_signal(
            barrier, inc=1, device_id=(lax.rem(me_c + i, n_ctx), me), device_id_type=MESH
        )

    heads = lp_ref.shape[1]
    for layer in range(n_ctx):
        lsend[layer, :, 0:heads] = jnp.broadcast_to(lp_ref[layer : layer + 1, :], (8, heads))
        lsend[layer, :, heads:] = jnp.zeros((8, LANES - heads), jnp.float32)

    lane16 = lax.broadcasted_iota(jnp.int32, (16, LANES), 1) < ROPE
    zero8 = jnp.zeros((8, LANES), jnp.float32)

    def make(t):
        p = chip_to(t)
        qs = pl.ds(pl.multiple_of(p * 384, 128), 384)
        ks = pl.ds(pl.multiple_of(p * 256, 128), 256)
        qv = (
            MOMENTUM_DECAY * qm_ref[:, qs].astype(jnp.float32) + qg_ref[:, qs].astype(jnp.float32)
        ).astype(jnp.bfloat16)
        kv = (
            MOMENTUM_DECAY * km_ref[:, ks].astype(jnp.float32) + kg_ref[:, ks].astype(jnp.float32)
        ).astype(jnp.bfloat16)
        qv_ref[:, qs] = qv
        kv_ref[:, ks] = kv
        qv = qv.astype(jnp.float32)
        kv = kv.astype(jnp.float32)
        middle = qv[:, 128:256]
        turned = half_roll(middle)
        low = jnp.concatenate([middle[16:24], zero8], axis=0)
        low_turned = jnp.concatenate([turned[16:24], zero8], axis=0)
        even = 2 * t + core
        odd = 2 * t + 1 - core
        send[even, 0:32, :] = jnp.concatenate([qv[:, 0:128], kv[:, 0:128]], axis=0).astype(
            jnp.bfloat16
        )
        send[even, 32:48, :] = jnp.where(lane16, middle[0:16], low_turned).astype(jnp.bfloat16)
        send[odd, 0:32, :] = jnp.concatenate([qv[:, 256:384], kv[:, 128:256]], axis=0).astype(
            jnp.bfloat16
        )
        send[odd, 32:48, :] = jnp.where(lane16, turned[0:16], low).astype(jnp.bfloat16)

    def out_copy(t, dc):
        j = 2 * t + dc
        return pltpu.make_async_remote_copy(
            src_ref=send.at[j],
            dst_ref=recv.at[j],
            send_sem=send_sem,
            recv_sem=recv_sem.at[lax.div(j, group)],
            device_id=(me_c, 2 * chip_to(t) + core_at(dc)),
            device_id_type=MESH,
        )

    def back_copy(t, dc):
        j = 2 * t + dc
        return pltpu.make_async_remote_copy(
            src_ref=back.at[j],
            dst_ref=home.at[j],
            send_sem=back_sem,
            recv_sem=home_sem.at[lax.div(j, group)],
            device_id=(me_c, 2 * chip_from(t) + core_at(dc)),
            device_id_type=MESH,
        )

    def span(buffer_out, buffer_in, first, size, out_sem, in_sem):
        return pltpu.make_async_remote_copy(
            src_ref=buffer_out.at[pl.ds(first, size)],
            dst_ref=buffer_in.at[pl.ds(first, size)],
            send_sem=out_sem,
            recv_sem=in_sem,
            device_id=(me_c, me),
            device_id_type=MESH,
        )

    make(0)
    recv[0] = send[0]
    pl.semaphore_wait(barrier, owners - 1 + n_ctx - 1)
    out_copy(0, 1).start()

    @pl.loop(1, chips)
    def _(t):
        make(t)
        out_copy(t, 0).start()
        out_copy(t, 1).start()

    @pl.loop(1, n_ctx)
    def _(i):
        other = lax.rem(me_c + i, n_ctx)
        pltpu.make_async_remote_copy(
            src_ref=lsend.at[other],
            dst_ref=lrecv.at[i],
            send_sem=lsend_sem,
            recv_sem=lrecv_sem,
            device_id=(other, me),
            device_id_type=MESH,
        ).start()

    rows = group * 32
    row = lax.rem(lax.broadcasted_iota(jnp.int32, (rows, LANES), 0), 32)
    is_query = row < 24
    lane = lax.broadcasted_iota(jnp.int32, (group * 16, LANES), 1) < ROPE

    def gather(k):
        first = pl.multiple_of(k * rows, rows)
        block = recv[pl.ds(k * group, group), 0:32, :].reshape(rows, LANES).astype(jnp.float32)
        third = recv[pl.ds(k * group, group), 32:48, :].reshape(group * 16, LANES)
        third = third.astype(jnp.float32)
        top = jnp.where(lane, third, 0.0).reshape(group, 16, LANES)
        bottom = jnp.where(lane, half_roll(third), 0.0).reshape(group, 16, LANES)
        third = jnp.concatenate([top, bottom], axis=1).reshape(rows, LANES)
        query = jnp.where(is_query, block, 0.0).astype(jnp.bfloat16)
        key = jnp.where(is_query, 0.0, block).astype(jnp.bfloat16)
        full = jnp.concatenate([query, third.astype(jnp.bfloat16)], axis=1)
        wide[pl.ds(first, rows), 0:256] = full
        wide[pl.ds(first, rows), 256:384] = key
        gram_q[...] += gram_of(full)
        gram_k[...] += gram_of(key)

    gram_q[...] = jnp.zeros_like(gram_q)
    gram_k[...] = jnp.zeros_like(gram_k)
    span(send, recv, 1, group - 1, send_sem, recv_sem.at[0]).wait_recv()
    gather(0)

    @pl.loop(1, groups)
    def _(k):
        span(send, recv, k * group, group, send_sem, recv_sem.at[k]).wait_recv()
        gather(k)

    mq, mk = newton(gram_q[...], gram_k[...])
    mq_high, mq_low = split(mq)
    mk_high, mk_low = split(mk)

    def give(k):
        first = pl.multiple_of(k * rows, rows)
        query = low_dot(wide[pl.ds(first, rows), 0:256], mq_high, mq_low)
        key = low_dot(wide[pl.ds(first, rows), 256:384], mk_high, mk_low)
        block = query[:, 0:128] + key
        third = query[:, 128:256].reshape(group, 32, LANES)
        top = third[:, 0:16].reshape(group * 16, LANES)
        bottom = half_roll(third[:, 16:32].reshape(group * 16, LANES))
        third = jnp.where(lane, top, bottom)
        back[pl.ds(k * group, group), 0:32, :] = block.astype(jnp.bfloat16).reshape(
            group, 32, LANES
        )
        back[pl.ds(k * group, group), 32:48, :] = third.astype(jnp.bfloat16).reshape(
            group, 16, LANES
        )

    give(0)
    back_copy(0, 1).start()
    for t in range(1, pairs):
        back_copy(t, 0).start()
        back_copy(t, 1).start()
    home[0] = back[0]

    @pl.loop(1, groups)
    def _(k):
        give(k)

        @pl.loop(0, pairs)
        def _(i):
            back_copy(k * pairs + i, 0).start()
            back_copy(k * pairs + i, 1).start()

    lrecv[0] = lsend[me_c]
    pltpu.make_async_remote_copy(
        src_ref=lsend.at[pl.ds(1, n_ctx - 1)],
        dst_ref=lrecv.at[pl.ds(1, n_ctx - 1)],
        send_sem=lsend_sem,
        recv_sem=lrecv_sem,
        device_id=(me_c, me),
        device_id_type=MESH,
    ).wait()
    rowmax = jnp.max(lrecv[...], axis=0)[0:1, 0:heads]
    order = order_ref[pl.ds(me_c, 1), :]
    hit = jnp.broadcast_to(order, (heads, heads)) == lax.broadcasted_iota(
        jnp.int32, (heads, heads), 0
    )
    logit_max = jnp.sum(
        jnp.where(hit, jnp.broadcast_to(rowmax, (heads, heads)), 0.0), axis=1, keepdims=True
    )
    clip = jnp.minimum(1.0, CLIP_LIMIT / logit_max)
    gamma[...] = jnp.broadcast_to(clip, (heads, LANES))
    root[...] = jnp.broadcast_to(jnp.sqrt(clip), (heads, LANES))

    load_q.wait()
    load_k.wait()
    keep = 1.0 - LEARN_RATE * WEIGHT_DECAY
    rate_q = LEARN_RATE * (0.2 * math.sqrt(max(QR, WIDTH)))
    rate_k = LEARN_RATE * (0.2 * math.sqrt(max(KR, NOPE)))
    lane1 = lax.broadcasted_iota(jnp.int32, (1, LANES), 1) < ROPE

    def finish(t):
        p = chip_to(t)
        even = home[2 * t + core].astype(jnp.float32)
        odd = home[2 * t + 1 - core].astype(jnp.float32)
        even_third, odd_third = even[32:48], odd[32:48]
        even_turned, odd_turned = half_roll(even_third), half_roll(odd_third)
        middle = jnp.concatenate(
            [
                jnp.where(lane16, even_third, odd_turned),
                jnp.where(lane16, even_turned, odd_third)[0:8],
            ],
            axis=0,
        )
        g_even, g_odd = gamma[pl.ds(2 * p, 1), :], gamma[pl.ds(2 * p + 1, 1), :]
        r_even, r_odd = root[pl.ds(2 * p, 1), :], root[pl.ds(2 * p + 1, 1), :]
        tiles = (
            (even[0:24], r_even),
            (middle, jnp.where(lane1, g_even, r_odd)),
            (odd[0:24], jnp.where(lane1, r_odd, g_odd)),
        )
        for i, (ortho, factor) in enumerate(tiles):
            at = pl.ds(pl.multiple_of(p * 384 + i * 128, 128), 128)
            qf_ref[:, at] = (qw_ref[:, at] * keep - rate_q * ortho) * factor
        for i, (ortho, factor) in enumerate(((even[24:32], r_even), (odd[24:32], r_odd))):
            at = pl.ds(pl.multiple_of(p * 256 + i * 128, 128), 128)
            kf_ref[:, at] = (kw_ref[:, at] * keep - rate_k * ortho) * factor

    span(back, home, 1, group - 1, back_sem, home_sem.at[0]).wait_recv()

    @pl.loop(0, pairs)
    def _(i):
        finish(i)

    @pl.loop(1, groups)
    def _(k):
        span(back, home, k * group, group, back_sem, home_sem.at[k]).wait_recv()

        @pl.loop(0, pairs)
        def _(i):
            finish(k * pairs + i)

    span(send, recv, 1, owners - 1, send_sem, recv_sem.at[0]).wait_send()
    span(back, home, 1, owners - 1, back_sem, home_sem.at[0]).wait_send()


def local(
    logit_partial,
    head_order,
    query_weight,
    query_moment,
    query_grad,
    key_weight,
    key_moment,
    key_grad,
):
    owners = lax.axis_size("zero")
    n_ctx = lax.axis_size("ctx")
    groups = owners // (8 if owners == 64 else 4)
    heads = head_order.shape[1]
    query, key = query_weight.shape[1:], key_weight.shape[1:]
    vmem = pl.BlockSpec(memory_space=pltpu.VMEM)
    hbm = pl.BlockSpec(memory_space=pl.ANY)
    dma = pltpu.SemaphoreType.DMA
    qf, qv, kf, kv = pl.pallas_call(
        functools.partial(body, owners, n_ctx),
        out_shape=(
            jax.ShapeDtypeStruct(query, jnp.float32),
            jax.ShapeDtypeStruct(query, jnp.bfloat16),
            jax.ShapeDtypeStruct(key, jnp.float32),
            jax.ShapeDtypeStruct(key, jnp.bfloat16),
        ),
        in_specs=[vmem, vmem, hbm, vmem, vmem, hbm, vmem, vmem],
        out_specs=(vmem, vmem, vmem, vmem),
        scratch_shapes=[
            pltpu.VMEM((owners, ROWS, LANES), jnp.bfloat16),
            pltpu.VMEM((owners, ROWS, LANES), jnp.bfloat16),
            pltpu.VMEM((owners, ROWS, LANES), jnp.bfloat16),
            pltpu.VMEM((owners, ROWS, LANES), jnp.bfloat16),
            pltpu.VMEM((owners * 32, 384), jnp.bfloat16),
            pltpu.VMEM((256, 256), jnp.float32),
            pltpu.VMEM((128, 128), jnp.float32),
            pltpu.VMEM((n_ctx, 8, LANES), jnp.float32),
            pltpu.VMEM((n_ctx, 8, LANES), jnp.float32),
            pltpu.VMEM((heads, LANES), jnp.float32),
            pltpu.VMEM((heads, LANES), jnp.float32),
            pltpu.VMEM(query, jnp.float32),
            pltpu.VMEM(key, jnp.float32),
            dma,
            dma((groups,)),
            dma,
            dma((groups,)),
            dma,
            dma,
            dma((2,)),
        ],
        compiler_params=pltpu.CompilerParams(
            collective_id=0, has_side_effects=True, vmem_limit_bytes=48 * 1024 * 1024
        ),
        name="muon",
    )(
        logit_partial[0],
        head_order,
        query_weight[0],
        query_moment[0],
        query_grad[0],
        key_weight[0],
        key_moment[0],
        key_grad[0],
    )
    return (qf[None], qv[None], kf[None], kv[None])


def solution(mesh):
    shard = P("ctx", "zero", None)
    return jax.shard_map(
        local,
        mesh=mesh,
        in_specs=(P("ctx", None, None), P(), shard, shard, shard, shard, shard, shard),
        out_specs=(shard, shard, shard, shard),
        check_vma=False,
    )
```

profile of v0, /device:TPU:1, one launch (start us, length us, event | category | flops | bytes accessed | tf_op | source)
XLA Modules:
  0.0 76.9 jit_solution(3937817153776988795)
XLA Ops:
  0.6 0.0 copy-start
  0.6 1.3 %copy-done = f32[1,24,12288]{2,1,0:T(8,128)S(1)} copy-done((f32[1,24,12288]{2,1,0:T(8,128)S(1)}, f32[1,24,12288]{2,1,0:T(8,128)}, u32[]{:S(2)}) %copy-start) | copy-done | bytes 1179672
  1.9 0.0 copy-start.1
  1.9 1.1 %copy-done.1 = bf16[1,24,12288]{2,1,0:T(8,128)(2,1)S(1)} copy-done((bf16[1,24,12288]{2,1,0:T(8,128)(2,1)S(1)}, bf16[1,24,12288]{2,1,0:T(8,128)(2,1)}, u32[]{:S(2)}) %copy-start.1) | copy-done | bytes 589848
  3.0 0.0 copy-start.2
  3.0 1.1 %copy-done.2 = bf16[1,24,12288]{2,1,0:T(8,128)(2,1)S(1)} copy-done((bf16[1,24,12288]{2,1,0:T(8,128)(2,1)S(1)}, bf16[1,24,12288]{2,1,0:T(8,128)(2,1)}, u32[]{:S(2)}) %copy-start.2) | copy-done | bytes 589848
  4.0 0.0 copy-start.3
  4.0 0.9 %copy-done.3 = f32[1,8,8192]{2,1,0:T(8,128)S(1)} copy-done((f32[1,8,8192]{2,1,0:T(8,128)S(1)}, f32[1,8,8192]{2,1,0:T(8,128)}, u32[]{:S(2)}) %copy-start.3) | copy-done | bytes 262168
  5.0 0.0 copy-start.4
  5.0 0.9 %copy-done.4 = bf16[1,8,8192]{2,1,0:T(8,128)(2,1)S(1)} copy-done((bf16[1,8,8192]{2,1,0:T(8,128)(2,1)S(1)}, bf16[1,8,8192]{2,1,0:T(8,128)(2,1)}, u32[]{:S(2)}) %copy-start.4) | copy-done | bytes 131096
  5.9 0.0 copy-start.5
  5.9 0.9 %copy-done.5 = bf16[1,8,8192]{2,1,0:T(8,128)(2,1)S(1)} copy-done((bf16[1,8,8192]{2,1,0:T(8,128)(2,1)S(1)}, bf16[1,8,8192]{2,1,0:T(8,128)(2,1)}, u32[]{:S(2)}) %copy-start.5) | copy-done | bytes 131096
  6.8 0.0 copy-start.6
  6.8 0.7 copy-done.6
  7.5 0.0 copy-start.7
  7.5 0.7 copy-done.7
  8.2 65.6 %muon.1 = (f32[24,12288]{1,0:T(8,128)S(1)}, bf16[24,12288]{1,0:T(8,128)(2,1)S(1)}, f32[8,8192]{1,0:T(8,128)S(1)}, bf16[8,8192]{1,0:T(8,128)(2,1)S(1)}) custom-call(f32[8,64]{1,0:T(8,128)S(1)} %bitcast.21, s32[8,64]{1,0:T(8,128)S(1)} %copy-done.7, f32[24,12288]{1,0:T(8,128)S(1)} %bitcast.11, bf16[24,12288]{1,0:T(8,128)(2,1)S(1)} %bitcast.14, ...), custom_call_target="tpu_custom_call" | custom-call | tf_op jit(solution)/shard_map/muon/pallas_call | solution.py:420
  73.8 1.0 %copy.16 = f32[1,24,12288]{2,1,0:T(8,128)} copy(f32[1,24,12288]{2,1,0:T(8,128)S(1)} %bitcast.12) | data formatting | bytes 2359296
  74.8 0.8 %copy.17 = bf16[1,24,12288]{2,1,0:T(8,128)(2,1)} copy(bf16[1,24,12288]{2,1,0:T(8,128)(2,1)S(1)} %bitcast.13) | data formatting | bytes 1179648
  75.6 0.7 copy.18
  76.3 0.7 copy.19
Async XLA Ops:
  0.6 1.3 %copy-start = (f32[1,24,12288]{2,1,0:T(8,128)S(1)}, f32[1,24,12288]{2,1,0:T(8,128)}, u32[]{:S(2)}) copy-start(f32[1,24,12288]{2,1,0:T(8,128)} %param.10) | copy-start | bytes 3538948
  1.9 1.1 %copy-start.1 = (bf16[1,24,12288]{2,1,0:T(8,128)(2,1)S(1)}, bf16[1,24,12288]{2,1,0:T(8,128)(2,1)}, u32[]{:S(2)}) copy-start(bf16[1,24,12288]{2,1,0:T(8,128)(2,1)} %param.11) | copy-start | bytes 1769476
  3.0 1.1 %copy-start.2 = (bf16[1,24,12288]{2,1,0:T(8,128)(2,1)S(1)}, bf16[1,24,12288]{2,1,0:T(8,128)(2,1)}, u32[]{:S(2)}) copy-start(bf16[1,24,12288]{2,1,0:T(8,128)(2,1)} %param.12) | copy-start | bytes 1769476
  4.0 0.9 %copy-start.3 = (f32[1,8,8192]{2,1,0:T(8,128)S(1)}, f32[1,8,8192]{2,1,0:T(8,128)}, u32[]{:S(2)}) copy-start(f32[1,8,8192]{2,1,0:T(8,128)} %param.13) | copy-start | bytes 786436
  5.0 0.9 %copy-start.4 = (bf16[1,8,8192]{2,1,0:T(8,128)(2,1)S(1)}, bf16[1,8,8192]{2,1,0:T(8,128)(2,1)}, u32[]{:S(2)}) copy-start(bf16[1,8,8192]{2,1,0:T(8,128)(2,1)} %param.14) | copy-start | bytes 393220
  5.9 0.9 %copy-start.5 = (bf16[1,8,8192]{2,1,0:T(8,128)(2,1)S(1)}, bf16[1,8,8192]{2,1,0:T(8,128)(2,1)}, u32[]{:S(2)}) copy-start(bf16[1,8,8192]{2,1,0:T(8,128)(2,1)} %param.15) | copy-start | bytes 393220
  6.8 0.7 copy-start.6
  7.5 0.7 copy-start.7
where the time goes:
time: 77.3 us; the launch traced here: 76.9 us
  Pallas kernels  65.6 us (85%)
  local copies, waits for them, and re-layouts  10.7 us (14%)
    pallas_call x1, Pallas kernels, local(): pl.pallas_call(functools.partial(body, owners, n_ctx), out_shape=(jax.Sha...  65.6 us
    unnamed x20, local copies, waits for them, and re-layouts  10.7 us

commit v1 on v0

--- a/solution.py
+++ b/solution.py
@@ -46,32 +46,22 @@
     )
 
 
-def begin(gram):
-    size = gram.shape[0]
-    eye = lax.broadcasted_iota(jnp.int32, (size, size), 0) == lax.broadcasted_iota(
-        jnp.int32, (size, size), 1
-    )
-    total = jnp.sum(jnp.where(eye, gram, 0.0))
-    inverse = 1.0 / (jnp.sqrt(jnp.full((1, 1), total)) + NORM_EPSILON)
+def begin(gram, size):
+    gram = gram[0:size]
+    eye = lax.broadcasted_iota(jnp.int32, gram.shape, 0) == lax.broadcasted_iota(
+        jnp.int32, gram.shape, 1
+    )
+    total = jnp.sum(jnp.where(eye, gram, 0.0), axis=1, keepdims=True)
+    total = jnp.sum(total, axis=0, keepdims=True)
+    inverse = 1.0 / (jnp.sqrt(total) + NORM_EPSILON)
     return gram * inverse * inverse, inverse, jnp.where(eye, 1.0, 0.0)
 
 
-def newton(gram_q, gram_k):
-    aq, iq, eq = begin(gram_q)
-    ak, ik, ek = begin(gram_k)
-    mq = mk = None
-    for sweep in range(ITERS):
-        sq, sk = mul(aq, aq), mul(ak, ak)
-        pq = NEWTON_FIRST * eq + NEWTON_SECOND * aq + NEWTON_THIRD * sq
-        pk = NEWTON_FIRST * ek + NEWTON_SECOND * ak + NEWTON_THIRD * sk
-        if sweep == 0:
-            mq, mk = pq, pk
-        else:
-            mq, mk = mul(mq, pq), mul(mk, pk)
-        if sweep < ITERS - 1:
-            yq, yk = mul(aq, pq), mul(ak, pk)
-            aq, ak = mul(yq, pq), mul(yk, pk)
-    return mq * iq, mk * ik
+def square(x):
+    missing = x.shape[1] - x.shape[0]
+    if not missing:
+        return x
+    return jnp.concatenate([x, jnp.zeros((missing, x.shape[1]), x.dtype)], axis=0)
 
 
 def split(m):
@@ -79,6 +69,46 @@
     return high, (m - high.astype(jnp.float32)).astype(jnp.bfloat16)
 
 
+def mul3(a, b):
+    b_high, b_low = square(b[0]), square(b[1])
+    return (
+        jnp.dot(a[0], b_high, preferred_element_type=jnp.float32)
+        + jnp.dot(a[0], b_low, preferred_element_type=jnp.float32)
+        + jnp.dot(a[1], b_high, preferred_element_type=jnp.float32)
+    )
+
+
+def stack(a, b):
+    return tuple(jnp.concatenate(pair, axis=0) for pair in zip(a, b))
+
+
+def newton(grams):
+    a, inverse, eye = (list(x) for x in zip(*grams))
+    m = [None] * len(a)
+    which = range(len(a))
+    for sweep in range(ITERS):
+        exact = sweep == 0
+        halves = [split(a[i]) for i in which]
+        if exact:
+            s = [mul(a[i], square(a[i])) for i in which]
+        else:
+            s = [mul3(halves[i], halves[i]) for i in which]
+        p = [NEWTON_FIRST * eye[i] + NEWTON_SECOND * a[i] + NEWTON_THIRD * s[i] for i in which]
+        p_halves = [split(p[i]) for i in which]
+        if exact:
+            y = [mul(a[i], square(p[i])) for i in which]
+            a = [mul(y[i], square(p[i])) for i in which]
+            m = p
+        elif sweep < ITERS - 1:
+            both = [mul3(stack(halves[i], split(m[i])), p_halves[i]) for i in which]
+            size = [a[i].shape[0] for i in which]
+            a = [mul3(split(both[i][0 : size[i]]), p_halves[i]) for i in which]
+            m = [both[i][size[i] :] for i in which]
+        else:
+            m = [mul3(split(m[i]), p_halves[i]) for i in which]
+    return [m[i] * inverse[i] for i in which]
+
+
 def half_roll(x):
     return pltpu.roll(x, ROPE, 1)
 
@@ -86,14 +116,14 @@
 def body(
     owners,
     n_ctx,
-    lp_ref,
-    order_ref,
+    lp_hbm,
+    order_hbm,
     qw_hbm,
-    qm_ref,
-    qg_ref,
+    qm_hbm,
+    qg_hbm,
     kw_hbm,
-    km_ref,
-    kg_ref,
+    km_hbm,
+    kg_hbm,
     qf_ref,
     qv_ref,
     kf_ref,
@@ -111,6 +141,12 @@
     root,
     qw_ref,
     kw_ref,
+    qm_ref,
+    qg_ref,
+    km_ref,
+    kg_ref,
+    lp_ref,
+    order_ref,
     send_sem,
     recv_sem,
     back_sem,
@@ -148,10 +184,23 @@
     def core_at(dc):
         return lax.rem(core + dc, 2)
 
-    load_q = pltpu.make_async_copy(qw_hbm, qw_ref, load_sem.at[0])
-    load_k = pltpu.make_async_copy(kw_hbm, kw_ref, load_sem.at[1])
-    load_q.start()
-    load_k.start()
+    loads = [
+        pltpu.make_async_copy(source, target, load_sem.at[i])
+        for i, (source, target) in enumerate(
+            (
+                (qm_hbm, qm_ref),
+                (qg_hbm, qg_ref),
+                (km_hbm, km_ref),
+                (kg_hbm, kg_ref),
+                (lp_hbm, lp_ref),
+                (order_hbm, order_ref),
+                (qw_hbm, qw_ref),
+                (kw_hbm, kw_ref),
+            )
+        )
+    ]
+    for load in loads:
+        load.start()
 
     barrier = pltpu.get_barrier_semaphore()
 
@@ -168,6 +217,8 @@
         )
 
     heads = lp_ref.shape[1]
+    for load in loads[:5]:
+        load.wait()
     for layer in range(n_ctx):
         lsend[layer, :, 0:heads] = jnp.broadcast_to(lp_ref[layer : layer + 1, :], (8, heads))
         lsend[layer, :, heads:] = jnp.zeros((8, LANES - heads), jnp.float32)
@@ -290,8 +341,8 @@
         span(send, recv, k * group, group, send_sem, recv_sem.at[k]).wait_recv()
         gather(k)
 
-    mq, mk = newton(gram_q[...], gram_k[...])
-    mq_high, mq_low = split(mq)
+    mq, mk = newton([begin(gram_q[...], WIDTH), begin(gram_k[...], NOPE)])
+    mq_high, mq_low = split(square(mq))
     mk_high, mk_low = split(mk)
 
     def give(k):
@@ -336,6 +387,7 @@
         device_id_type=MESH,
     ).wait()
     rowmax = jnp.max(lrecv[...], axis=0)[0:1, 0:heads]
+    loads[5].wait()
     order = order_ref[pl.ds(me_c, 1), :]
     hit = jnp.broadcast_to(order, (heads, heads)) == lax.broadcasted_iota(
         jnp.int32, (heads, heads), 0
@@ -347,8 +399,8 @@
     gamma[...] = jnp.broadcast_to(clip, (heads, LANES))
     root[...] = jnp.broadcast_to(jnp.sqrt(clip), (heads, LANES))
 
-    load_q.wait()
-    load_k.wait()
+    for load in loads[6:]:
+        load.wait()
     keep = 1.0 - LEARN_RATE * WEIGHT_DECAY
     rate_q = LEARN_RATE * (0.2 * math.sqrt(max(QR, WIDTH)))
     rate_k = LEARN_RATE * (0.2 * math.sqrt(max(KR, NOPE)))
@@ -374,29 +426,41 @@
             (middle, jnp.where(lane1, g_even, r_odd)),
             (odd[0:24], jnp.where(lane1, r_odd, g_odd)),
         )
+        done = []
         for i, (ortho, factor) in enumerate(tiles):
             at = pl.ds(pl.multiple_of(p * 384 + i * 128, 128), 128)
-            qf_ref[:, at] = (qw_ref[:, at] * keep - rate_q * ortho) * factor
+            done.append((qf_ref, at, (qw_ref[:, at] * keep - rate_q * ortho) * factor))
         for i, (ortho, factor) in enumerate(((even[24:32], r_even), (odd[24:32], r_odd))):
             at = pl.ds(pl.multiple_of(p * 256 + i * 128, 128), 128)
-            kf_ref[:, at] = (kw_ref[:, at] * keep - rate_k * ortho) * factor
+            done.append((kf_ref, at, (kw_ref[:, at] * keep - rate_k * ortho) * factor))
+        return done
+
+    def finish_group(k):
+        done = []
+        for i in range(pairs):
+            done += finish(k * pairs + i)
+        for ref, at, value in done:
+            ref[:, at] = value
 
     span(back, home, 1, group - 1, back_sem, home_sem.at[0]).wait_recv()
-
-    @pl.loop(0, pairs)
-    def _(i):
-        finish(i)
+    finish_group(0)
 
     @pl.loop(1, groups)
     def _(k):
         span(back, home, k * group, group, back_sem, home_sem.at[k]).wait_recv()
-
-        @pl.loop(0, pairs)
-        def _(i):
-            finish(k * pairs + i)
+        finish_group(k)
 
     span(send, recv, 1, owners - 1, send_sem, recv_sem.at[0]).wait_send()
     span(back, home, 1, owners - 1, back_sem, home_sem.at[0]).wait_send()
+
+
+def emit(*refs):
+    sem = refs[8]
+    copies = [pltpu.make_async_copy(refs[i], refs[4 + i], sem.at[i]) for i in range(4)]
+    for copy in copies:
+        copy.start()
+    for copy in copies:
+        copy.wait()
 
 
 def local(
@@ -415,17 +479,18 @@
     heads = head_order.shape[1]
     query, key = query_weight.shape[1:], key_weight.shape[1:]
     vmem = pl.BlockSpec(memory_space=pltpu.VMEM)
-    hbm = pl.BlockSpec(memory_space=pl.ANY)
+    hbm = pl.BlockSpec(memory_space=pltpu.HBM)
     dma = pltpu.SemaphoreType.DMA
-    qf, qv, kf, kv = pl.pallas_call(
+    shapes = (
+        jax.ShapeDtypeStruct(query, jnp.float32),
+        jax.ShapeDtypeStruct(query, jnp.bfloat16),
+        jax.ShapeDtypeStruct(key, jnp.float32),
+        jax.ShapeDtypeStruct(key, jnp.bfloat16),
+    )
+    results = pl.pallas_call(
         functools.partial(body, owners, n_ctx),
-        out_shape=(
-            jax.ShapeDtypeStruct(query, jnp.float32),
-            jax.ShapeDtypeStruct(query, jnp.bfloat16),
-            jax.ShapeDtypeStruct(key, jnp.float32),
-            jax.ShapeDtypeStruct(key, jnp.bfloat16),
-        ),
-        in_specs=[vmem, vmem, hbm, vmem, vmem, hbm, vmem, vmem],
+        out_shape=shapes,
+        in_specs=[hbm] * 8,
         out_specs=(vmem, vmem, vmem, vmem),
         scratch_shapes=[
             pltpu.VMEM((owners, ROWS, LANES), jnp.bfloat16),
@@ -441,29 +506,48 @@
             pltpu.VMEM((heads, LANES), jnp.float32),
             pltpu.VMEM(query, jnp.float32),
             pltpu.VMEM(key, jnp.float32),
+            pltpu.VMEM(query, jnp.bfloat16),
+            pltpu.VMEM(query, jnp.bfloat16),
+            pltpu.VMEM(key, jnp.bfloat16),
+            pltpu.VMEM(key, jnp.bfloat16),
+            pltpu.VMEM(logit_partial.shape[1:], jnp.float32),
+            pltpu.VMEM(head_order.shape, jnp.int32),
             dma,
             dma((groups,)),
             dma,
             dma((groups,)),
             dma,
             dma,
-            dma((2,)),
+            dma((8,)),
         ],
         compiler_params=pltpu.CompilerParams(
             collective_id=0, has_side_effects=True, vmem_limit_bytes=48 * 1024 * 1024
         ),
         name="muon",
     )(
-        logit_partial[0],
-        head_order,
-        query_weight[0],
-        query_moment[0],
-        query_grad[0],
-        key_weight[0],
-        key_moment[0],
-        key_grad[0],
-    )
-    return (qf[None], qv[None], kf[None], kv[None])
+        *(
+            pltpu.with_memory_space_constraint(array, pltpu.HBM)
+            for array in (
+                logit_partial[0],
+                head_order,
+                query_weight[0],
+                query_moment[0],
+                query_grad[0],
+                key_weight[0],
+                key_moment[0],
+                key_grad[0],
+            )
+        )
+    )
+    results = pl.pallas_call(
+        emit,
+        out_shape=shapes,
+        in_specs=[vmem] * 4,
+        out_specs=[hbm] * 4,
+        scratch_shapes=[dma((4,))],
+        name="emit",
+    )(*results)
+    return tuple(result[None] for result in results)
 
 
 def solution(mesh):

time: 77.3 us -> 69.2 us (0.90)
  local copies, waits for them, and re-layouts: 10.7 us -> 3.21 us
    unnamed x20 -> x8, local copies, waits for them, and re-layouts: 10.7 us -> 3.21 us
    pallas_call x1 -> x2, Pallas kernels: 65.6 us -> 65.2 us  [the longest x1 62.3 us: local(): pl.pallas_call(functools.partial(body, owners, n_ctx), out_shape=shapes,...]
where the time goes in v1:
time: 69.2 us; the launch traced here: 69.1 us
  Pallas kernels  65.2 us (94%)
  local copies, waits for them, and re-layouts  3.21 us (5%)
    pallas_call x1, Pallas kernels, local(): pl.pallas_call(functools.partial(body, owners, n_ctx), out_shape=shapes,...  62.3 us
    unnamed x8, local copies, waits for them, and re-layouts  3.21 us
    pallas_call x1, Pallas kernels, local(): pl.pallas_call(emit, out_shape=shapes, in_specs=[vmem] * 4, out_specs=[hb...  2.87 us

profile of v1, /device:TPU:1, one launch (start us, length us, event | category | flops | bytes accessed | tf_op | source)
XLA Modules:
  0.0 69.1 jit_solution(17402753244911522097)
XLA Ops:
  0.6 62.3 %muon.1 = (f32[24,12288]{1,0:T(8,128)S(1)}, bf16[24,12288]{1,0:T(8,128)(2,1)S(1)}, f32[8,8192]{1,0:T(8,128)S(1)}, bf16[8,8192]{1,0:T(8,128)(2,1)S(1)}) custom-call(f32[8,64]{1,0:T(8,128)} %bitcast.17, s32[8,64]{1,0:T(8,128)} %order_hbm.1, f32[24,12288]{1,0:T(8,128)} %bitcast.11, bf16[24,12288]{1,0:T(8,128)(2,1)} %bitcast.12, bf16[24,12288]{1,0:T(8,128)(2,1)} %bitcast.13, ...), custom_call_target="tpu_custom_call" | custom-call | tf_op jit(solution)/shard_map/muon/pallas_call | solution.py:490
  63.0 0.0 copy-start
  63.0 1.0 %copy-done = f32[24,12288]{1,0:T(8,128)} copy-done((f32[24,12288]{1,0:T(8,128)}, f32[24,12288]{1,0:T(8,128)S(1)}, u32[]{:S(2)}) %copy-start) | copy-done | bytes 1179672
  64.0 0.0 copy-start.1
  64.0 0.8 %copy-done.1 = bf16[24,12288]{1,0:T(8,128)(2,1)} copy-done((bf16[24,12288]{1,0:T(8,128)(2,1)}, bf16[24,12288]{1,0:T(8,128)(2,1)S(1)}, u32[]{:S(2)}) %copy-start.1) | copy-done | bytes 589848
  64.8 0.0 copy-start.2
  64.8 0.7 %copy-done.2 = f32[8,8192]{1,0:T(8,128)} copy-done((f32[8,8192]{1,0:T(8,128)}, f32[8,8192]{1,0:T(8,128)S(1)}, u32[]{:S(2)}) %copy-start.2) | copy-done | bytes 262168
  65.5 0.0 copy-start.3
  65.5 0.7 copy-done.3
  66.2 2.9 %emit.1 = (f32[24,12288]{1,0:T(8,128)}, bf16[24,12288]{1,0:T(8,128)(2,1)}, f32[8,8192]{1,0:T(8,128)}, bf16[8,8192]{1,0:T(8,128)(2,1)}) custom-call(f32[24,12288]{1,0:T(8,128)} %copy-done, bf16[24,12288]{1,0:T(8,128)(2,1)} %copy-done.1, f32[8,8192]{1,0:T(8,128)} %copy-done.2, bf16[8,8192]{1,0:T(8,128)(2,1)} %copy-done.3), custom_call_target="tpu_custom_call" | custom-call | tf_op jit(solution)/shard_map/emit/pallas_call | solution.py:542
Async XLA Ops:
  63.0 1.0 %copy-start = (f32[24,12288]{1,0:T(8,128)}, f32[24,12288]{1,0:T(8,128)S(1)}, u32[]{:S(2)}) copy-start(f32[24,12288]{1,0:T(8,128)S(1)} %get-tuple-element.12.refs_0_) | copy-start | bytes 3538948
  64.0 0.8 %copy-start.1 = (bf16[24,12288]{1,0:T(8,128)(2,1)}, bf16[24,12288]{1,0:T(8,128)(2,1)S(1)}, u32[]{:S(2)}) copy-start(bf16[24,12288]{1,0:T(8,128)(2,1)S(1)} %get-tuple-element.13.refs_1_) | copy-start | bytes 1769476
  64.8 0.7 %copy-start.2 = (f32[8,8192]{1,0:T(8,128)}, f32[8,8192]{1,0:T(8,128)S(1)}, u32[]{:S(2)}) copy-start(f32[8,8192]{1,0:T(8,128)S(1)} %get-tuple-element.14.refs_2_) | copy-start | bytes 786436
  65.5 0.7 copy-start.3

commit v2 on v1

--- a/solution.py
+++ b/solution.py
@@ -132,6 +132,8 @@
     recv,
     back,
     home,
+    relay,
+    relay_back,
     wide,
     gram_q,
     gram_k,
@@ -151,6 +153,7 @@
     recv_sem,
     back_sem,
     home_sem,
+    relay_sem,
     lsend_sem,
     lrecv_sem,
     load_sem,
@@ -158,9 +161,11 @@
     nx = 4 if owners == 64 else 1
     chips = owners // 2
     nz = chips // nx
-    group = 8 if owners == 64 else 4
+    group = 2 * nx
     groups = owners // group
     pairs = group // 2
+    direct = nx * (nz - 1)
+    quarter = nz // 4
     me_c = lax.axis_index("ctx")
     me = lax.axis_index("zero")
     core = lax.rem(me, 2)
@@ -168,9 +173,11 @@
     x0, z0 = lax.div(chip, nz), lax.rem(chip, nz)
 
     def offset(t):
-        i = lax.rem(t, nz)
+        if isinstance(t, int) and t >= direct:
+            return t - direct, 2 * quarter
+        i = lax.rem(t, nz - 1)
         dz = lax.div(i + 1, 2) * (1 - 2 * lax.rem(i + 1, 2))
-        dx = lax.rem(t + lax.div(t, nz), nx)
+        dx = lax.rem(i + lax.div(t, nz - 1), nx)
         return dx, dz
 
     def chip_to(t):
@@ -287,16 +294,56 @@
             device_id_type=MESH,
         )
 
+    opposite = [(dx, dc) for dx in range(nx) for dc in range(2)]
+
+    def aside(dx, dc):
+        step = quarter if (dx + dc) % 2 == 0 else nz - quarter
+        return lax.rem(z0 + step, nz)
+
+    def first_leg(source, target, out_sem, in_sem, sign):
+        for dx, dc in opposite:
+            j = 2 * (direct + dx) + dc
+            x = lax.rem(x0 + nx + sign * dx, nx)
+            pltpu.make_async_remote_copy(
+                src_ref=source.at[j],
+                dst_ref=target.at[2 * dx + dc],
+                send_sem=out_sem,
+                recv_sem=in_sem,
+                device_id=(me_c, 2 * (x * nz + aside(dx, dc)) + core_at(dc)),
+                device_id_type=MESH,
+            ).start()
+
+    def second_leg(source, target, out_sem, in_sem):
+        for dx, dc in opposite:
+            j = 2 * (direct + dx) + dc
+            pltpu.make_async_remote_copy(
+                src_ref=source.at[2 * dx + dc],
+                dst_ref=target.at[j],
+                send_sem=out_sem,
+                recv_sem=in_sem,
+                device_id=(me_c, 2 * (x0 * nz + aside(dx, dc)) + core),
+                device_id_type=MESH,
+            ).start()
+
     make(0)
     recv[0] = send[0]
+    for dx in range(nx):
+        make(direct + dx)
     pl.semaphore_wait(barrier, owners - 1 + n_ctx - 1)
+    first_leg(send, relay, send_sem, relay_sem.at[0], 1)
     out_copy(0, 1).start()
 
-    @pl.loop(1, chips)
-    def _(t):
-        make(t)
-        out_copy(t, 0).start()
-        out_copy(t, 1).start()
+    def send_some(first, last):
+        @pl.loop(first, last)
+        def _(t):
+            make(t)
+            out_copy(t, 0).start()
+            out_copy(t, 1).start()
+
+    send_some(1, direct // 2)
+    span(relay, relay, 0, group, send_sem, relay_sem.at[0]).wait_recv()
+    second_leg(relay, recv, relay_sem.at[1], recv_sem.at[groups - 1])
+    send_some(direct // 2, direct)
 
     @pl.loop(1, n_ctx)
     def _(i):
@@ -361,6 +408,8 @@
             group, 16, LANES
         )
 
+    give(groups - 1)
+    first_leg(back, relay_back, back_sem, relay_sem.at[2], -1)
     give(0)
     back_copy(0, 1).start()
     for t in range(1, pairs):
@@ -368,14 +417,20 @@
         back_copy(t, 1).start()
     home[0] = back[0]
 
-    @pl.loop(1, groups)
-    def _(k):
-        give(k)
-
-        @pl.loop(0, pairs)
-        def _(i):
-            back_copy(k * pairs + i, 0).start()
-            back_copy(k * pairs + i, 1).start()
+    def give_some(first, last):
+        @pl.loop(first, last)
+        def _(k):
+            give(k)
+
+            @pl.loop(0, pairs)
+            def _(i):
+                back_copy(k * pairs + i, 0).start()
+                back_copy(k * pairs + i, 1).start()
+
+    give_some(1, groups // 2)
+    span(relay_back, relay_back, 0, group, back_sem, relay_sem.at[2]).wait_recv()
+    second_leg(relay_back, home, relay_sem.at[3], home_sem.at[groups - 1])
+    give_some(groups // 2, groups - 1)
 
     lrecv[0] = lsend[me_c]
     pltpu.make_async_remote_copy(
@@ -445,11 +500,17 @@
     span(back, home, 1, group - 1, back_sem, home_sem.at[0]).wait_recv()
     finish_group(0)
 
-    @pl.loop(1, groups)
+    @pl.loop(1, groups - 1)
     def _(k):
         span(back, home, k * group, group, back_sem, home_sem.at[k]).wait_recv()
         finish_group(k)
 
+    last = (groups - 1) * group
+    span(back, home, last, group, back_sem, home_sem.at[groups - 1]).wait_recv()
+    finish_group(groups - 1)
+
+    span(relay, relay, 0, group, relay_sem.at[1], relay_sem.at[0]).wait_send()
+    span(relay_back, relay_back, 0, group, relay_sem.at[3], relay_sem.at[2]).wait_send()
     span(send, recv, 1, owners - 1, send_sem, recv_sem.at[0]).wait_send()
     span(back, home, 1, owners - 1, back_sem, home_sem.at[0]).wait_send()
 
@@ -475,7 +536,8 @@
 ):
     owners = lax.axis_size("zero")
     n_ctx = lax.axis_size("ctx")
-    groups = owners // (8 if owners == 64 else 4)
+    group = 8 if owners == 64 else 2
+    groups = owners // group
     heads = head_order.shape[1]
     query, key = query_weight.shape[1:], key_weight.shape[1:]
     vmem = pl.BlockSpec(memory_space=pltpu.VMEM)
@@ -497,6 +559,8 @@
             pltpu.VMEM((owners, ROWS, LANES), jnp.bfloat16),
             pltpu.VMEM((owners, ROWS, LANES), jnp.bfloat16),
             pltpu.VMEM((owners, ROWS, LANES), jnp.bfloat16),
+            pltpu.VMEM((group, ROWS, LANES), jnp.bfloat16),
+            pltpu.VMEM((group, ROWS, LANES), jnp.bfloat16),
             pltpu.VMEM((owners * 32, 384), jnp.bfloat16),
             pltpu.VMEM((256, 256), jnp.float32),
             pltpu.VMEM((128, 128), jnp.float32),
@@ -516,6 +580,7 @@
             dma((groups,)),
             dma,
             dma((groups,)),
+            dma((4,)),
             dma,
             dma,
             dma((8,)),
@@ -545,8 +610,9 @@
         in_specs=[vmem] * 4,
         out_specs=[hbm] * 4,
         scratch_shapes=[dma((4,))],
+        compiler_params=pltpu.CompilerParams(vmem_limit_bytes=8 * 1024 * 1024),
         name="emit",
-    )(*results)
+    )(*(pltpu.with_memory_space_constraint(result, pltpu.VMEM) for result in results))
     return tuple(result[None] for result in results)
 
 

time: 69.2 us -> 64.5 us (0.932)
  local copies, waits for them, and re-layouts: 3.21 us -> 0 us
  Pallas kernels: 65.2 us -> 63.7 us
    unnamed x8 -> x0, local copies, waits for them, and re-layouts: 3.21 us -> none
    pallas_call x1, Pallas kernels: 2.87 us -> 1.36 us  [local(): pl.pallas_call(emit, out_shape=shapes, in_specs=[vmem] * 4, out_specs=[hb...]
where the time goes in v2:
time: 64.5 us; the launch traced here: 64.3 us
  Pallas kernels  63.7 us (99%)
    pallas_call x1, Pallas kernels, local(): pl.pallas_call(functools.partial(body, owners, n_ctx), out_shape=shapes,...  62.3 us
    pallas_call x1, Pallas kernels, local(): pl.pallas_call(emit, out_shape=shapes, in_specs=[vmem] * 4, out_specs=[hb...  1.36 us

profile of v2, /device:TPU:1, one launch (start us, length us, event | category | flops | bytes accessed | tf_op | source)
XLA Modules:
  0.0 64.3 jit_solution(13417786790127740531)
XLA Ops:
  0.6 62.3 %muon.1 = (f32[24,12288]{1,0:T(8,128)S(1)}, bf16[24,12288]{1,0:T(8,128)(2,1)S(1)}, f32[8,8192]{1,0:T(8,128)S(1)}, bf16[8,8192]{1,0:T(8,128)(2,1)S(1)}) custom-call(f32[8,64]{1,0:T(8,128)} %bitcast.17, s32[8,64]{1,0:T(8,128)} %order_hbm.1, f32[24,12288]{1,0:T(8,128)} %bitcast.11, bf16[24,12288]{1,0:T(8,128)(2,1)} %bitcast.12, bf16[24,12288]{1,0:T(8,128)(2,1)} %bitcast.13, ...), custom_call_target="tpu_custom_call" | custom-call | tf_op jit(solution)/shard_map/muon/pallas_call | solution.py:552
  63.0 1.4 %emit.1 = (f32[24,12288]{1,0:T(8,128)}, bf16[24,12288]{1,0:T(8,128)(2,1)}, f32[8,8192]{1,0:T(8,128)}, bf16[8,8192]{1,0:T(8,128)(2,1)}) custom-call(f32[24,12288]{1,0:T(8,128)S(1)} %get-tuple-element.12.refs_0_, bf16[24,12288]{1,0:T(8,128)(2,1)S(1)} %get-tuple-element.13.refs_1_, f32[8,8192]{1,0:T(8,128)S(1)} %get-tuple-element.14.refs_2_, ...), custom_call_target="tpu_custom_call" | custom-call | tf_op jit(solution)/shard_map/emit/pallas_call | solution.py:607

commit v3 on v1

--- a/solution.py
+++ b/solution.py
@@ -158,7 +158,7 @@
     nx = 4 if owners == 64 else 1
     chips = owners // 2
     nz = chips // nx
-    group = 8 if owners == 64 else 4
+    group = 2 * nx
     groups = owners // group
     pairs = group // 2
     me_c = lax.axis_index("ctx")
@@ -167,22 +167,24 @@
     chip = lax.div(me, 2)
     x0, z0 = lax.div(chip, nz), lax.rem(chip, nz)
 
+    def core_at(dc):
+        return lax.rem(core + dc, 2)
+
     def offset(t):
         i = lax.rem(t, nz)
         dz = lax.div(i + 1, 2) * (1 - 2 * lax.rem(i + 1, 2))
-        dx = lax.rem(t + lax.div(t, nz), nx)
+        dx = lax.rem(i + lax.div(t, nz), nx)
         return dx, dz
 
     def chip_to(t):
         dx, dz = offset(t)
-        return lax.rem(x0 + dx, nx) * nz + lax.rem(z0 + dz + nz, nz)
-
-    def chip_from(t):
+        way = 1 - 2 * core
+        return lax.rem(x0 + way * dx + nx, nx) * nz + lax.rem(z0 + way * dz + nz, nz)
+
+    def chip_from(t, dc):
         dx, dz = offset(t)
-        return lax.rem(x0 - dx + nx, nx) * nz + lax.rem(z0 - dz + nz, nz)
-
-    def core_at(dc):
-        return lax.rem(core + dc, 2)
+        way = 1 - 2 * core_at(dc)
+        return lax.rem(x0 - way * dx + nx, nx) * nz + lax.rem(z0 - way * dz + nz, nz)
 
     loads = [
         pltpu.make_async_copy(source, target, load_sem.at[i])
@@ -273,7 +275,7 @@
             dst_ref=home.at[j],
             send_sem=back_sem,
             recv_sem=home_sem.at[lax.div(j, group)],
-            device_id=(me_c, 2 * chip_from(t) + core_at(dc)),
+            device_id=(me_c, 2 * chip_from(t, dc) + core_at(dc)),
             device_id_type=MESH,
         )
 
@@ -475,7 +477,8 @@
 ):
     owners = lax.axis_size("zero")
     n_ctx = lax.axis_size("ctx")
-    groups = owners // (8 if owners == 64 else 4)
+    group = 8 if owners == 64 else 2
+    groups = owners // group
     heads = head_order.shape[1]
     query, key = query_weight.shape[1:], key_weight.shape[1:]
     vmem = pl.BlockSpec(memory_space=pltpu.VMEM)
@@ -545,8 +548,9 @@
         in_specs=[vmem] * 4,
         out_specs=[hbm] * 4,
         scratch_shapes=[dma((4,))],
+        compiler_params=pltpu.CompilerParams(vmem_limit_bytes=8 * 1024 * 1024),
         name="emit",
-    )(*results)
+    )(*(pltpu.with_memory_space_constraint(result, pltpu.VMEM) for result in results))
     return tuple(result[None] for result in results)
 
 

time: 69.2 us -> 64.8 us (0.936)
  local copies, waits for them, and re-layouts: 3.21 us -> 0 us
  Pallas kernels: 65.2 us -> 64 us
    unnamed x8 -> x0, local copies, waits for them, and re-layouts: 3.21 us -> none
    pallas_call x1, Pallas kernels: 2.87 us -> 1.36 us  [local(): pl.pallas_call(emit, out_shape=shapes, in_specs=[vmem] * 4, out_specs=[hb...]
where the time goes in v3:
time: 64.8 us; the launch traced here: 64.6 us
  Pallas kernels  64 us (99%)
    pallas_call x1, Pallas kernels, local(): pl.pallas_call(functools.partial(body, owners, n_ctx), out_shape=shapes,...  62.6 us
    pallas_call x1, Pallas kernels, local(): pl.pallas_call(emit, out_shape=shapes, in_specs=[vmem] * 4, out_specs=[hb...  1.36 us

profile of v3, /device:TPU:1, one launch (start us, length us, event | category | flops | bytes accessed | tf_op | source)
XLA Modules:
  0.0 64.6 jit_solution(11268611954652541478)
XLA Ops:
  0.6 62.6 %muon.1 = (f32[24,12288]{1,0:T(8,128)S(1)}, bf16[24,12288]{1,0:T(8,128)(2,1)S(1)}, f32[8,8192]{1,0:T(8,128)S(1)}, bf16[8,8192]{1,0:T(8,128)(2,1)S(1)}) custom-call(f32[8,64]{1,0:T(8,128)} %bitcast.17, s32[8,64]{1,0:T(8,128)} %order_hbm.1, f32[24,12288]{1,0:T(8,128)} %bitcast.11, bf16[24,12288]{1,0:T(8,128)(2,1)} %bitcast.12, bf16[24,12288]{1,0:T(8,128)(2,1)} %bitcast.13, ...), custom_call_target="tpu_custom_call" | custom-call | tf_op jit(solution)/shard_map/muon/pallas_call | solution.py:493
  63.2 1.4 %emit.1 = (f32[24,12288]{1,0:T(8,128)}, bf16[24,12288]{1,0:T(8,128)(2,1)}, f32[8,8192]{1,0:T(8,128)}, bf16[8,8192]{1,0:T(8,128)(2,1)}) custom-call(f32[24,12288]{1,0:T(8,128)S(1)} %get-tuple-element.12.refs_0_, bf16[24,12288]{1,0:T(8,128)(2,1)S(1)} %get-tuple-element.13.refs_1_, f32[8,8192]{1,0:T(8,128)S(1)} %get-tuple-element.14.refs_2_, ...), custom_call_target="tpu_custom_call" | custom-call | tf_op jit(solution)/shard_map/emit/pallas_call | solution.py:545

commit v4 on v3

--- a/solution.py
+++ b/solution.py
@@ -34,18 +34,6 @@
     return lax.dot_general(x, x, (((0,), (0,)), ((), ())), preferred_element_type=jnp.float32)
 
 
-def mul(a, b):
-    return lax.dot_general(
-        a, b, (((1,), (0,)), ((), ())), precision=HIGHEST, preferred_element_type=jnp.float32
-    )
-
-
-def low_dot(x, high, low):
-    return jnp.dot(x, high, preferred_element_type=jnp.float32) + jnp.dot(
-        x, low, preferred_element_type=jnp.float32
-    )
-
-
 def begin(gram, size):
     gram = gram[0:size]
     eye = lax.broadcasted_iota(jnp.int32, gram.shape, 0) == lax.broadcasted_iota(
@@ -69,13 +57,27 @@
     return high, (m - high.astype(jnp.float32)).astype(jnp.bfloat16)
 
 
+def split3(m):
+    high = m.astype(jnp.bfloat16)
+    rest = m - high.astype(jnp.float32)
+    middle = rest.astype(jnp.bfloat16)
+    return high, middle, (rest - middle.astype(jnp.float32)).astype(jnp.bfloat16)
+
+
+def joined(lefts, rights):
+    return jnp.dot(
+        jnp.concatenate(lefts, axis=1),
+        jnp.concatenate([square(right) for right in rights], axis=0),
+        preferred_element_type=jnp.float32,
+    )
+
+
 def mul3(a, b):
-    b_high, b_low = square(b[0]), square(b[1])
-    return (
-        jnp.dot(a[0], b_high, preferred_element_type=jnp.float32)
-        + jnp.dot(a[0], b_low, preferred_element_type=jnp.float32)
-        + jnp.dot(a[1], b_high, preferred_element_type=jnp.float32)
-    )
+    return joined((a[0], a[0], a[1]), (b[0], b[1], b[0]))
+
+
+def mul6(a, b):
+    return joined((a[0], a[0], a[1], a[1], a[0], a[2]), (b[0], b[1], b[0], b[1], b[2], b[0]))
 
 
 def stack(a, b):
@@ -88,24 +90,22 @@
     which = range(len(a))
     for sweep in range(ITERS):
         exact = sweep == 0
-        halves = [split(a[i]) for i in which]
+        parts, product = (split3, mul6) if exact else (split, mul3)
+        a_parts = [parts(a[i]) for i in which]
+        s = [product(a_parts[i], a_parts[i]) for i in which]
+        p = [NEWTON_FIRST * eye[i] + NEWTON_SECOND * a[i] + NEWTON_THIRD * s[i] for i in which]
+        p_parts = [parts(p[i]) for i in which]
         if exact:
-            s = [mul(a[i], square(a[i])) for i in which]
-        else:
-            s = [mul3(halves[i], halves[i]) for i in which]
-        p = [NEWTON_FIRST * eye[i] + NEWTON_SECOND * a[i] + NEWTON_THIRD * s[i] for i in which]
-        p_halves = [split(p[i]) for i in which]
-        if exact:
-            y = [mul(a[i], square(p[i])) for i in which]
-            a = [mul(y[i], square(p[i])) for i in which]
+            y = [product(a_parts[i], p_parts[i]) for i in which]
+            a = [product(parts(y[i]), p_parts[i]) for i in which]
             m = p
         elif sweep < ITERS - 1:
-            both = [mul3(stack(halves[i], split(m[i])), p_halves[i]) for i in which]
+            both = [product(stack(a_parts[i], parts(m[i])), p_parts[i]) for i in which]
             size = [a[i].shape[0] for i in which]
-            a = [mul3(split(both[i][0 : size[i]]), p_halves[i]) for i in which]
+            a = [product(parts(both[i][0 : size[i]]), p_parts[i]) for i in which]
             m = [both[i][size[i] :] for i in which]
         else:
-            m = [mul3(split(m[i]), p_halves[i]) for i in which]
+            m = [product(parts(m[i]), p_parts[i]) for i in which]
     return [m[i] * inverse[i] for i in which]
 
 
@@ -133,6 +133,7 @@
     back,
     home,
     wide,
+    factor,
     gram_q,
     gram_k,
     lsend,
@@ -201,7 +202,7 @@
             )
         )
     ]
-    for load in loads:
+    for load in loads[:6]:
         load.start()
 
     barrier = pltpu.get_barrier_semaphore()
@@ -219,12 +220,10 @@
         )
 
     heads = lp_ref.shape[1]
-    for load in loads[:5]:
+    for load in loads[:4]:
         load.wait()
-    for layer in range(n_ctx):
-        lsend[layer, :, 0:heads] = jnp.broadcast_to(lp_ref[layer : layer + 1, :], (8, heads))
-        lsend[layer, :, heads:] = jnp.zeros((8, LANES - heads), jnp.float32)
-
+    for load in loads[6:]:
+        load.start()
     lane16 = lax.broadcasted_iota(jnp.int32, (16, LANES), 1) < ROPE
     zero8 = jnp.zeros((8, LANES), jnp.float32)
 
@@ -300,6 +299,11 @@
         out_copy(t, 0).start()
         out_copy(t, 1).start()
 
+    loads[4].wait()
+    for layer in range(n_ctx):
+        lsend[layer, :, 0:heads] = jnp.broadcast_to(lp_ref[layer : layer + 1, :], (8, heads))
+        lsend[layer, :, heads:] = jnp.zeros((8, LANES - heads), jnp.float32)
+
     @pl.loop(1, n_ctx)
     def _(i):
         other = lax.rem(me_c + i, n_ctx)
@@ -344,15 +348,21 @@
         gather(k)
 
     mq, mk = newton([begin(gram_q[...], WIDTH), begin(gram_k[...], NOPE)])
-    mq_high, mq_low = split(square(mq))
-    mk_high, mk_low = split(mk)
+    mq, mk = split(square(mq)), split(mk)
+    for half in range(2):
+        first = half * 384
+        factor[first : first + 256, :] = mq[half]
+        factor[first + 256 : first + 384, 0:128] = mk[half]
+        factor[first + 256 : first + 384, 128:256] = jnp.zeros((128, 128), jnp.bfloat16)
 
     def give(k):
         first = pl.multiple_of(k * rows, rows)
-        query = low_dot(wide[pl.ds(first, rows), 0:256], mq_high, mq_low)
-        key = low_dot(wide[pl.ds(first, rows), 256:384], mk_high, mk_low)
-        block = query[:, 0:128] + key
-        third = query[:, 128:256].reshape(group, 32, LANES)
+        x = wide[pl.ds(first, rows), :]
+        product = jnp.dot(
+            jnp.concatenate([x, x], axis=1), factor[...], preferred_element_type=jnp.float32
+        )
+        block = product[:, 0:128]
+        third = product[:, 128:256].reshape(group, 32, LANES)
         top = third[:, 0:16].reshape(group * 16, LANES)
         bottom = half_roll(third[:, 16:32].reshape(group * 16, LANES))
         third = jnp.where(lane, top, bottom)
@@ -501,6 +511,7 @@
             pltpu.VMEM((owners, ROWS, LANES), jnp.bfloat16),
             pltpu.VMEM((owners, ROWS, LANES), jnp.bfloat16),
             pltpu.VMEM((owners * 32, 384), jnp.bfloat16),
+            pltpu.VMEM((768, 256), jnp.bfloat16),
             pltpu.VMEM((256, 256), jnp.float32),
             pltpu.VMEM((128, 128), jnp.float32),
             pltpu.VMEM((n_ctx, 8, LANES), jnp.float32),

time: 64.8 us -> 64.7 us (level)
  no operation moved by 1% of the time
where the time goes in v4:
time: 64.7 us; the launch traced here: 64.6 us
  Pallas kernels  63.9 us (99%)
    pallas_call x1, Pallas kernels, local(): pl.pallas_call(functools.partial(body, owners, n_ctx), out_shape=shapes,...  62.5 us
    pallas_call x1, Pallas kernels, local(): pl.pallas_call(emit, out_shape=shapes, in_specs=[vmem] * 4, out_specs=[hb...  1.36 us

profile of v4, /device:TPU:1, one launch (start us, length us, event | category | flops | bytes accessed | tf_op | source)
XLA Modules:
  0.0 64.6 jit_solution(3396337470494858796)
XLA Ops:
  0.6 62.5 %muon.1 = (f32[24,12288]{1,0:T(8,128)S(1)}, bf16[24,12288]{1,0:T(8,128)(2,1)S(1)}, f32[8,8192]{1,0:T(8,128)S(1)}, bf16[8,8192]{1,0:T(8,128)(2,1)S(1)}) custom-call(f32[8,64]{1,0:T(8,128)} %bitcast.17, s32[8,64]{1,0:T(8,128)} %order_hbm.1, f32[24,12288]{1,0:T(8,128)} %bitcast.11, bf16[24,12288]{1,0:T(8,128)(2,1)} %bitcast.12, bf16[24,12288]{1,0:T(8,128)(2,1)} %bitcast.13, ...), custom_call_target="tpu_custom_call" | custom-call | tf_op jit(solution)/shard_map/muon/pallas_call | solution.py:503
  63.2 1.4 %emit.1 = (f32[24,12288]{1,0:T(8,128)}, bf16[24,12288]{1,0:T(8,128)(2,1)}, f32[8,8192]{1,0:T(8,128)}, bf16[8,8192]{1,0:T(8,128)(2,1)}) custom-call(f32[24,12288]{1,0:T(8,128)S(1)} %get-tuple-element.12.refs_0_, bf16[24,12288]{1,0:T(8,128)(2,1)S(1)} %get-tuple-element.13.refs_1_, f32[8,8192]{1,0:T(8,128)S(1)} %get-tuple-element.14.refs_2_, ...), custom_call_target="tpu_custom_call" | custom-call | tf_op jit(solution)/shard_map/emit/pallas_call | solution.py:556

commit v5 on v4

--- a/solution.py
+++ b/solution.py
@@ -172,9 +172,10 @@
         return lax.rem(core + dc, 2)
 
     def offset(t):
-        i = lax.rem(t, nz)
+        far = lax.rem(chips - t, chips)
+        i = lax.div(far, nx)
         dz = lax.div(i + 1, 2) * (1 - 2 * lax.rem(i + 1, 2))
-        dx = lax.rem(i + lax.div(t, nz), nx)
+        dx = lax.rem(far, nx)
         return dx, dz
 
     def chip_to(t):

time: 64.7 us -> 63.6 us (0.983)
  Pallas kernels: 63.9 us -> 62.8 us
    pallas_call x1, Pallas kernels: 62.5 us -> 61.5 us  [local(): pl.pallas_call(functools.partial(body, owners, n_ctx), out_shape=shapes,...]
where the time goes in v5:
time: 63.6 us; the launch traced here: 63.5 us
  Pallas kernels  62.8 us (99%)
  between operations  0.64 us (1%)
    pallas_call x1, Pallas kernels, local(): pl.pallas_call(functools.partial(body, owners, n_ctx), out_shape=shapes,...  61.5 us
    pallas_call x1, Pallas kernels, local(): pl.pallas_call(emit, out_shape=shapes, in_specs=[vmem] * 4, out_specs=[hb...  1.36 us

profile of v5, /device:TPU:1, one launch (start us, length us, event | category | flops | bytes accessed | tf_op | source)
XLA Modules:
  0.0 63.5 jit_solution(3403389489798597613)
XLA Ops:
  0.6 61.5 %muon.1 = (f32[24,12288]{1,0:T(8,128)S(1)}, bf16[24,12288]{1,0:T(8,128)(2,1)S(1)}, f32[8,8192]{1,0:T(8,128)S(1)}, bf16[8,8192]{1,0:T(8,128)(2,1)S(1)}) custom-call(f32[8,64]{1,0:T(8,128)} %bitcast.17, s32[8,64]{1,0:T(8,128)} %order_hbm.1, f32[24,12288]{1,0:T(8,128)} %bitcast.11, bf16[24,12288]{1,0:T(8,128)(2,1)} %bitcast.12, bf16[24,12288]{1,0:T(8,128)(2,1)} %bitcast.13, ...), custom_call_target="tpu_custom_call" | custom-call | tf_op jit(solution)/shard_map/muon/pallas_call | solution.py:504
  62.1 1.4 %emit.1 = (f32[24,12288]{1,0:T(8,128)}, bf16[24,12288]{1,0:T(8,128)(2,1)}, f32[8,8192]{1,0:T(8,128)}, bf16[8,8192]{1,0:T(8,128)(2,1)}) custom-call(f32[24,12288]{1,0:T(8,128)S(1)} %get-tuple-element.12.refs_0_, bf16[24,12288]{1,0:T(8,128)(2,1)S(1)} %get-tuple-element.13.refs_1_, f32[8,8192]{1,0:T(8,128)S(1)} %get-tuple-element.14.refs_2_, ...), custom_call_target="tpu_custom_call" | custom-call | tf_op jit(solution)/shard_map/emit/pallas_call | solution.py:557

commit v6 on v5

--- a/solution.py
+++ b/solution.py
@@ -78,10 +78,6 @@
 
 def mul6(a, b):
     return joined((a[0], a[0], a[1], a[1], a[0], a[2]), (b[0], b[1], b[0], b[1], b[2], b[0]))
-
-
-def stack(a, b):
-    return tuple(jnp.concatenate(pair, axis=0) for pair in zip(a, b))
 
 
 def newton(grams):
@@ -100,10 +96,9 @@
             a = [product(parts(y[i]), p_parts[i]) for i in which]
             m = p
         elif sweep < ITERS - 1:
-            both = [product(stack(a_parts[i], parts(m[i])), p_parts[i]) for i in which]
-            size = [a[i].shape[0] for i in which]
-            a = [product(parts(both[i][0 : size[i]]), p_parts[i]) for i in which]
-            m = [both[i][size[i] :] for i in which]
+            y = [product(a_parts[i], p_parts[i]) for i in which]
+            m = [product(parts(m[i]), p_parts[i]) for i in which]
+            a = [product(parts(y[i]), p_parts[i]) for i in which]
         else:
             m = [product(parts(m[i]), p_parts[i]) for i in which]
     return [m[i] * inverse[i] for i in which]

time: 63.6 us -> 63.3 us (level)
  no operation moved by 1% of the time
where the time goes in v6:
time: 63.3 us; the launch traced here: 63.2 us
  Pallas kernels  62.6 us (99%)
  between operations  0.64 us (1%)
    pallas_call x1, Pallas kernels, local(): pl.pallas_call(functools.partial(body, owners, n_ctx), out_shape=shapes,...  61.2 us
    pallas_call x1, Pallas kernels, local(): pl.pallas_call(emit, out_shape=shapes, in_specs=[vmem] * 4, out_specs=[hb...  1.36 us

profile of v6, /device:TPU:1, one launch (start us, length us, event | category | flops | bytes accessed | tf_op | source)
XLA Modules:
  0.0 63.2 jit_solution(17514957869005579153)
XLA Ops:
  0.6 61.2 %muon.1 = (f32[24,12288]{1,0:T(8,128)S(1)}, bf16[24,12288]{1,0:T(8,128)(2,1)S(1)}, f32[8,8192]{1,0:T(8,128)S(1)}, bf16[8,8192]{1,0:T(8,128)(2,1)S(1)}) custom-call(f32[8,64]{1,0:T(8,128)} %bitcast.17, s32[8,64]{1,0:T(8,128)} %order_hbm.1, f32[24,12288]{1,0:T(8,128)} %bitcast.11, bf16[24,12288]{1,0:T(8,128)(2,1)} %bitcast.12, bf16[24,12288]{1,0:T(8,128)(2,1)} %bitcast.13, ...), custom_call_target="tpu_custom_call" | custom-call | tf_op jit(solution)/shard_map/muon/pallas_call | solution.py:499
  61.8 1.4 %emit.1 = (f32[24,12288]{1,0:T(8,128)}, bf16[24,12288]{1,0:T(8,128)(2,1)}, f32[8,8192]{1,0:T(8,128)}, bf16[8,8192]{1,0:T(8,128)(2,1)}) custom-call(f32[24,12288]{1,0:T(8,128)S(1)} %get-tuple-element.12.refs_0_, bf16[24,12288]{1,0:T(8,128)(2,1)S(1)} %get-tuple-element.13.refs_1_, f32[8,8192]{1,0:T(8,128)S(1)} %get-tuple-element.14.refs_2_, ...), custom_call_target="tpu_custom_call" | custom-call | tf_op jit(solution)/shard_map/emit/pallas_call | solution.py:552
